TPU v7x, 32 devices: a whole 2x2x4 slice. The times are simulated.
32 devices in a mesh: loop: 8 (over z, core), group: 4 (over y, x).
Axes of the slice: x: 2, y: 2, z: 4, core: 2. Of those that a mesh axis runs over, the one named last changes fastest.
Arguments:
- node_feats: bfloat16 [16384, 512], P(('loop', 'group')), may hold values from -64 to 64
- w_qkv: bfloat16 [512, 8, 192], P(None, 'group'), may hold values from -1 to 1
- w_out: bfloat16 [512, 512], P('group'), may hold values from -0.25 to 0.25
- tile_cols: int32 [128, 10], P('loop'), may hold values from 0 to 127, as said below
Outputs:
- attended: bfloat16 [16384, 512], P(('loop', 'group'))
Inputs may be any that keep to these rules, and one draw needn't show every extreme that they name: `tile_cols`: each row names 10 distinct tiles, among them the row's own tile b; exactly 4 of them lie in the row's own node block of 16 tiles, and each of the others lies in a different other node block. Rows of one node block that name tiles of the same other node block name different tiles of it.
All inputs are finite; a program needn't handle non-finite values.
Results may differ from a plain program's by a relative error of at most 0.019.
Values may be sent and summed in bfloat16 or wider, within the bound.
A program may use at most 128 MiB of HBM per device.

v0:
```python
import jax
import jax.numpy as jnp
from jax import lax
from jax.sharding import PartitionSpec as P

TILE = 128
MOST = 4


NEG_FILL = -1e30


def passed_along(value, axis, by):
    peers = lax.axis_size(axis)
    return lax.ppermute(value, axis, [(i, (i + by) % peers) for i in range(peers)])


def gather_tiles(kv_block, chosen):
    tiles_here = kv_block.shape[0] // TILE
    blocks = kv_block.reshape(tiles_here, TILE, kv_block.shape[1], kv_block.shape[2])
    picked = blocks[chosen]
    return picked.reshape(
        chosen.shape[0], chosen.shape[1] * TILE, kv_block.shape[1], kv_block.shape[2]
    )


def absorb(carried, queries, kv_block, owner_shard, local_idx, source):
    maxima, denom, accum = carried
    head_dim = queries.shape[-1]
    eligible = owner_shard == source
    running_rank = jnp.cumsum(eligible.astype(jnp.int32), axis=1) - 1
    slot_ids = jnp.arange(MOST, dtype=jnp.int32)
    hits = eligible[:, :, None] & (running_rank[:, :, None] == slot_ids[None, None, :])
    chosen = jnp.sum(jnp.where(hits, local_idx[:, :, None], 0), axis=1)
    present = jnp.any(hits, axis=1)
    kv_tiles = gather_tiles(kv_block, chosen)
    scores = jnp.einsum(
        "bqhe,bjhe->bhqj", queries, kv_tiles[..., :head_dim], preferred_element_type=jnp.float32
    ) * (1.0 / head_dim**0.5)
    keep = jnp.repeat(present, TILE, axis=1)[:, None, None, :]
    scores = jnp.where(keep, scores, NEG_FILL)
    new_max = jnp.maximum(maxima, jnp.max(scores, axis=-1))
    rescale = jnp.exp(maxima - new_max)
    weights = jnp.where(keep, jnp.exp(scores - new_max[..., None]), 0.0)
    denom = denom * rescale + jnp.sum(weights, axis=-1)
    accum = accum * rescale[..., None] + jnp.einsum(
        "bhqj,bjhe->bhqe",
        weights.astype(jnp.bfloat16),
        kv_tiles[..., head_dim:],
        preferred_element_type=jnp.float32,
    )
    return (new_max, denom, accum)


def per_device(node_feats, w_qkv, w_out, tile_cols):
    heads_here = w_qkv.shape[1]
    head_dim = w_qkv.shape[2] // 3
    projected = jnp.einsum(
        "nd,dhe->nhe",
        lax.all_gather(node_feats, "group", axis=0, tiled=True),
        w_qkv,
        preferred_element_type=jnp.float32,
    ).astype(jnp.bfloat16)
    rows_here = projected.shape[0]
    tiles_here = rows_here // TILE
    loop_size = lax.axis_size("loop")
    my_block = lax.axis_index("loop")
    queries = projected[:, :, :head_dim].reshape(tiles_here, TILE, heads_here, head_dim)
    keyvals = projected[:, :, head_dim:]
    owner_shard = tile_cols // tiles_here
    local_idx = tile_cols % tiles_here
    start_state = (
        jnp.full((tiles_here, heads_here, TILE), NEG_FILL, jnp.float32),
        jnp.zeros((tiles_here, heads_here, TILE), jnp.float32),
        jnp.zeros((tiles_here, heads_here, TILE, head_dim), jnp.float32),
    )
    carried = absorb(start_state, queries, keyvals, owner_shard, local_idx, my_block)

    def one_turn(turn, loop_carry):
        running, current = loop_carry
        current = passed_along(current, "loop", 1)
        running = absorb(
            running, queries, current, owner_shard, local_idx, (my_block - turn) % loop_size
        )
        return (running, current)

    carried, current = lax.fori_loop(1, loop_size, one_turn, (carried, keyvals))
    maxima, denom, accum = carried
    mixed = (accum / denom[..., None]).astype(jnp.bfloat16)
    mixed = jnp.transpose(mixed, (0, 2, 1, 3)).reshape(rows_here, heads_here * head_dim)
    return lax.psum_scatter(
        jnp.dot(mixed, w_out, preferred_element_type=jnp.float32).astype(jnp.bfloat16),
        "group",
        scatter_dimension=0,
        tiled=True,
    )


def solution(mesh):
    placed = (P(("loop", "group"), None), P(None, "group", None), P("group", None), P("loop", None))
    return jax.shard_map(
        per_device,
        mesh=mesh,
        in_specs=placed,
        out_specs=P(("loop", "group"), None),
        check_vma=False,
    )
```

profile of v0, /device:TPU:0, one launch (start us, length us, event | category | flops | bytes accessed | tf_op | source)
XLA Modules:
  0.0 386.9 jit_solution(16691810103468764150)
XLA Ops:
  9.8 37.5 %all-gather.2.cloned.1.call-done = bf16[2048,512]{1,0:T(8,128)(2,1)} async-done(((bf16[512,512]{1,0:T(8,128)(2,1)}), bf16[2048,512]{1,0:T(8,128)(2,1)}) %all-gather.2.cloned.1.call-update) | async-done | bytes 2097168 | tf_op jit(solution)/shard_map/all_gather | solution.py:60
  69.1 4.0 %fusion.38 = f32[16,2,128,64]{2,3,1,0:T(8,128)S(1)} fusion(bf16[16,512,2,64]{3,1,0,2:T(8,128)(2,1)S(1)} %copy-done.2, f32[16,2,128,512]{3,2,1,0:T(8,128)S(1)} %get-tuple-element.309, f32[16,2,128]{2,1,0:T(2,128)S(1)} %broadcast_maximum_fusion, pred[16,512]{1,0:T(8,128)(4,1)} %bitcast.118, f32[16,2,128]{2,1,0:T(2,128)S(1)} %get-tuple-element.306), kind=kOutput, calls=%fused_computation.49 | convolution fusion | flops 279183360 | bytes 11575296 | tf_op jit(solution)/shard_map/bhqj,bjhe->bhqe/dot_general | solution.py:46
  73.2 270.0 %while.21 = (s32[]{:T(128)}, f32[16,2,128]{2,1,0:T(2,128)S(1)}, f32[16,2,128]{2,1,0:T(2,128)}, f32[16,2,128,64]{2,3,1,0:T(8,128)S(1)}, bf16[2048,2,128]{2,0,1:T(...) while((s32[]{:T(128)}, f32[16,2,128]{2,1,0:T(2,128)S(1)}, ...), condition=%wide.region_11.12_spmd, body=%wide.region_5.11_spmd.sunk | while | flops 564673856 | bytes 67957664 | solution.py:87
  73.8 15.7 %collective-permute-done = bf16[2048,2,128]{2,0,1:T(8,128)(2,1)S(1)} collective-permute-done((bf16[2048,2,128]{2,0,1:T(8,128)(2,1)}, bf16[2048,2,128]{2,0,1:T(8,128)(2,1)S(1)}, u32[]{:S(2)}, u32[]{:S(2)}) %collective-permute-start) | collective-permute-done | bytes 1048608 | tf_op jit(solution)/shard_map/while/body/eval_jaxpr/ppermute | solution.py:15
  89.6 3.0 gather_fusion
  99.5 3.0 fusion.77
  103.9 7.0 %fusion.78 = f32[16,2,128,64]{2,3,1,0:T(8,128)S(1)} fusion(f32[16,2,512,128]{3,2,1,0:T(8,128)S(1)} %get-tuple-element.383, f32[16,2,128]{2,1,0:T(2,128)S(1)} %max.11, pred[16,512]{1,0:T(8,128)(4,1)S(1)} %bitcast.112, bf16[16,512,2,64]{3,1,0,2:T(8,128)(2,1)S(1)} %get-tuple-element.386, f32[16,2,128,64]{2,3,1,0:T(8,128)S(1)} %get-tuple-element.403, ...), kind=kOutput, calls=%fused_computation.19.clone.1 | convolution fusion | flops 279445504 | bytes 12623872 | tf_op jit(solution)/shard_map/while/body/eval_jaxpr/bhqj,bjhe->bhqe/dot_general | solution.py:46
  112.3 15.7 %collective-permute-done = bf16[2048,2,128]{2,0,1:T(8,128)(2,1)S(1)} collective-permute-done((bf16[2048,2,128]{2,0,1:T(8,128)(2,1)}, bf16[2048,2,128]{2,0,1:T(8,128)(2,1)S(1)}, u32[]{:S(2)}, u32[]{:S(2)}) %collective-permute-start) | collective-permute-done | bytes 1048608 | tf_op jit(solution)/shard_map/while/body/eval_jaxpr/ppermute | solution.py:15
  128.1 3.0 gather_fusion
  138.1 3.0 fusion.77
  142.4 7.0 %fusion.78 = f32[16,2,128,64]{2,3,1,0:T(8,128)S(1)} fusion(f32[16,2,512,128]{3,2,1,0:T(8,128)S(1)} %get-tuple-element.383, f32[16,2,128]{2,1,0:T(2,128)S(1)} %max.11, pred[16,512]{1,0:T(8,128)(4,1)S(1)} %bitcast.112, bf16[16,512,2,64]{3,1,0,2:T(8,128)(2,1)S(1)} %get-tuple-element.386, f32[16,2,128,64]{2,3,1,0:T(8,128)S(1)} %get-tuple-element.403, ...), kind=kOutput, calls=%fused_computation.19.clone.1 | convolution fusion | flops 279445504 | bytes 12623872 | tf_op jit(solution)/shard_map/while/body/eval_jaxpr/bhqj,bjhe->bhqe/dot_general | solution.py:46
  150.9 15.7 %collective-permute-done = bf16[2048,2,128]{2,0,1:T(8,128)(2,1)S(1)} collective-permute-done((bf16[2048,2,128]{2,0,1:T(8,128)(2,1)}, bf16[2048,2,128]{2,0,1:T(8,128)(2,1)S(1)}, u32[]{:S(2)}, u32[]{:S(2)}) %collective-permute-start) | collective-permute-done | bytes 1048608 | tf_op jit(solution)/shard_map/while/body/eval_jaxpr/ppermute | solution.py:15
  166.7 3.0 gather_fusion
  176.6 3.0 fusion.77
  181.0 7.0 %fusion.78 = f32[16,2,128,64]{2,3,1,0:T(8,128)S(1)} fusion(f32[16,2,512,128]{3,2,1,0:T(8,128)S(1)} %get-tuple-element.383, f32[16,2,128]{2,1,0:T(2,128)S(1)} %max.11, pred[16,512]{1,0:T(8,128)(4,1)S(1)} %bitcast.112, bf16[16,512,2,64]{3,1,0,2:T(8,128)(2,1)S(1)} %get-tuple-element.386, f32[16,2,128,64]{2,3,1,0:T(8,128)S(1)} %get-tuple-element.403, ...), kind=kOutput, calls=%fused_computation.19.clone.1 | convolution fusion | flops 279445504 | bytes 12623872 | tf_op jit(solution)/shard_map/while/body/eval_jaxpr/bhqj,bjhe->bhqe/dot_general | solution.py:46
  189.4 15.7 %collective-permute-done = bf16[2048,2,128]{2,0,1:T(8,128)(2,1)S(1)} collective-permute-done((bf16[2048,2,128]{2,0,1:T(8,128)(2,1)}, bf16[2048,2,128]{2,0,1:T(8,128)(2,1)S(1)}, u32[]{:S(2)}, u32[]{:S(2)}) %collective-permute-start) | collective-permute-done | bytes 1048608 | tf_op jit(solution)/shard_map/while/body/eval_jaxpr/ppermute | solution.py:15
  205.3 3.0 gather_fusion
  215.2 3.0 fusion.77
  219.6 7.0 %fusion.78 = f32[16,2,128,64]{2,3,1,0:T(8,128)S(1)} fusion(f32[16,2,512,128]{3,2,1,0:T(8,128)S(1)} %get-tuple-element.383, f32[16,2,128]{2,1,0:T(2,128)S(1)} %max.11, pred[16,512]{1,0:T(8,128)(4,1)S(1)} %bitcast.112, bf16[16,512,2,64]{3,1,0,2:T(8,128)(2,1)S(1)} %get-tuple-element.386, f32[16,2,128,64]{2,3,1,0:T(8,128)S(1)} %get-tuple-element.403, ...), kind=kOutput, calls=%fused_computation.19.clone.1 | convolution fusion | flops 279445504 | bytes 12623872 | tf_op jit(solution)/shard_map/while/body/eval_jaxpr/bhqj,bjhe->bhqe/dot_general | solution.py:46
  228.0 15.7 %collective-permute-done = bf16[2048,2,128]{2,0,1:T(8,128)(2,1)S(1)} collective-permute-done((bf16[2048,2,128]{2,0,1:T(8,128)(2,1)}, bf16[2048,2,128]{2,0,1:T(8,128)(2,1)S(1)}, u32[]{:S(2)}, u32[]{:S(2)}) %collective-permute-start) | collective-permute-done | bytes 1048608 | tf_op jit(solution)/shard_map/while/body/eval_jaxpr/ppermute | solution.py:15
  243.8 3.0 gather_fusion
  253.8 3.0 fusion.77
  258.1 7.0 %fusion.78 = f32[16,2,128,64]{2,3,1,0:T(8,128)S(1)} fusion(f32[16,2,512,128]{3,2,1,0:T(8,128)S(1)} %get-tuple-element.383, f32[16,2,128]{2,1,0:T(2,128)S(1)} %max.11, pred[16,512]{1,0:T(8,128)(4,1)S(1)} %bitcast.112, bf16[16,512,2,64]{3,1,0,2:T(8,128)(2,1)S(1)} %get-tuple-element.386, f32[16,2,128,64]{2,3,1,0:T(8,128)S(1)} %get-tuple-element.403, ...), kind=kOutput, calls=%fused_computation.19.clone.1 | convolution fusion | flops 279445504 | bytes 12623872 | tf_op jit(solution)/shard_map/while/body/eval_jaxpr/bhqj,bjhe->bhqe/dot_general | solution.py:46
  266.6 15.7 %collective-permute-done = bf16[2048,2,128]{2,0,1:T(8,128)(2,1)S(1)} collective-permute-done((bf16[2048,2,128]{2,0,1:T(8,128)(2,1)}, bf16[2048,2,128]{2,0,1:T(8,128)(2,1)S(1)}, u32[]{:S(2)}, u32[]{:S(2)}) %collective-permute-start) | collective-permute-done | bytes 1048608 | tf_op jit(solution)/shard_map/while/body/eval_jaxpr/ppermute | solution.py:15
  282.4 3.0 gather_fusion
  292.3 3.0 fusion.77
  296.7 7.0 %fusion.78 = f32[16,2,128,64]{2,3,1,0:T(8,128)S(1)} fusion(f32[16,2,512,128]{3,2,1,0:T(8,128)S(1)} %get-tuple-element.383, f32[16,2,128]{2,1,0:T(2,128)S(1)} %max.11, pred[16,512]{1,0:T(8,128)(4,1)S(1)} %bitcast.112, bf16[16,512,2,64]{3,1,0,2:T(8,128)(2,1)S(1)} %get-tuple-element.386, f32[16,2,128,64]{2,3,1,0:T(8,128)S(1)} %get-tuple-element.403, ...), kind=kOutput, calls=%fused_computation.19.clone.1 | convolution fusion | flops 279445504 | bytes 12623872 | tf_op jit(solution)/shard_map/while/body/eval_jaxpr/bhqj,bjhe->bhqe/dot_general | solution.py:46
  305.1 15.7 %collective-permute-done = bf16[2048,2,128]{2,0,1:T(8,128)(2,1)S(1)} collective-permute-done((bf16[2048,2,128]{2,0,1:T(8,128)(2,1)}, bf16[2048,2,128]{2,0,1:T(8,128)(2,1)S(1)}, u32[]{:S(2)}, u32[]{:S(2)}) %collective-permute-start) | collective-permute-done | bytes 1048608 | tf_op jit(solution)/shard_map/while/body/eval_jaxpr/ppermute | solution.py:15
  321.0 3.0 gather_fusion
  330.9 3.0 fusion.77
  335.3 7.0 %fusion.78 = f32[16,2,128,64]{2,3,1,0:T(8,128)S(1)} fusion(f32[16,2,512,128]{3,2,1,0:T(8,128)S(1)} %get-tuple-element.383, f32[16,2,128]{2,1,0:T(2,128)S(1)} %max.11, pred[16,512]{1,0:T(8,128)(4,1)S(1)} %bitcast.112, bf16[16,512,2,64]{3,1,0,2:T(8,128)(2,1)S(1)} %get-tuple-element.386, f32[16,2,128,64]{2,3,1,0:T(8,128)S(1)} %get-tuple-element.403, ...), kind=kOutput, calls=%fused_computation.19.clone.1 | convolution fusion | flops 279445504 | bytes 12623872 | tf_op jit(solution)/shard_map/while/body/eval_jaxpr/bhqj,bjhe->bhqe/dot_general | solution.py:46
  347.5 32.6 %reduce-scatter.2.cloned.1.call-done = bf16[512,512]{1,0:T(8,128)(2,1)} async-done(((bf16[2048,512]{1,0:T(8,128)(2,1)}), bf16[512,512]{1,0:T(8,128)(2,1)}) %reduce-scatter.2.cloned.1.call-update) | async-done | bytes 524304 | tf_op jit(solution)/shard_map/reduce_scatter | solution.py:91
  (209 shorter events, 97.5 us)
Async XLA Ops:
  6.5 40.7 %copy-start = (bf16[512,2,192]{0,2,1:T(8,128)(2,1)S(1)}, bf16[512,2,192]{0,2,1:T(8,128)(2,1)}, u32[]{:S(2)}) copy-start(bf16[512,2,192]{0,2,1:T(8,128)(2,1)} %param.7) | copy-start | bytes 1179652
  6.5 40.7 %all-gather.2.cloned.1.call-start = ((), (), s32[]{:S(2)}) async-start(), calls=%async_computation.1 | async-start | bytes 2621440 | tf_op jit(solution)/shard_map/all_gather | solution.py:60
  7.3 372.8 %reduce-scatter.2.cloned.1.call-start = ((), (), s32[]{:S(2)}) async-start(), calls=%async_computation.2 | async-start | bytes 2621440 | tf_op jit(solution)/shard_map/reduce_scatter | solution.py:91
  8.7 0.6 copy-start.4
  9.8 56.2 %copy-start.7 = (pred[2,8,4,128]{3,1,2,0:T(8,128)(4,1)}, pred[2,8,4,128]{3,1,2,0:T(8,128)(4,1)S(1)}, u32[]{:S(2)}) copy-start(pred[2,8,4,128]{3,1,2,0:T(8,128)(4,1)S(1)} %copy.111) | copy-start | bytes 24580
  66.0 3.2 copy-start.2
  69.1 4.0 %copy-start.5 = (s32[16,10]{0,1:T(8,128)S(1)}, s32[16,10]{0,1:T(8,128)}, u32[]{:S(2)}) copy-start(s32[16,10]{0,1:T(8,128)} %copy-done.4) | copy-start | bytes 1924
  69.1 4.0 %copy-start.6 = (s32[16,10]{0,1:T(8,128)S(1)}, s32[16,10]{0,1:T(8,128)}, u32[]{:S(2)}) copy-start(s32[16,10]{0,1:T(8,128)} %get-tuple-element.393) | copy-start | bytes 1924
  73.2 16.3 %collective-permute-start = (bf16[2048,2,128]{2,0,1:T(8,128)(2,1)}, bf16[2048,2,128]{2,0,1:T(8,128)(2,1)S(1)}, u32[]{:S(2)}, u32[]{:S(2)}) collective-permute-start(bf16[2048,2,128]{2,0,1:T(8,128)(2,1)} %get-tuple-element.404), channel_id=1, source_target_pairs={{0,4},{4,8},{8,12},{12,16},{16,20},{20,24},{24,28},{28,0},{1,5},{5... | collective-permute-start | bytes 3145736 | tf_op jit(solution)/shard_map/while/body/eval_jaxpr/ppermute | solution.py:15
  95.3 1.7 copy-start.3
  111.8 16.2 %collective-permute-start = (bf16[2048,2,128]{2,0,1:T(8,128)(2,1)}, bf16[2048,2,128]{2,0,1:T(8,128)(2,1)S(1)}, u32[]{:S(2)}, u32[]{:S(2)}) collective-permute-start(bf16[2048,2,128]{2,0,1:T(8,128)(2,1)} %get-tuple-element.404), channel_id=1, source_target_pairs={{0,4},{4,8},{8,12},{12,16},{16,20},{20,24},{24,28},{28,0},{1,5},{5... | collective-permute-start | bytes 3145736 | tf_op jit(solution)/shard_map/while/body/eval_jaxpr/ppermute | solution.py:15
  133.8 1.7 copy-start.3
  150.4 16.2 %collective-permute-start = (bf16[2048,2,128]{2,0,1:T(8,128)(2,1)}, bf16[2048,2,128]{2,0,1:T(8,128)(2,1)S(1)}, u32[]{:S(2)}, u32[]{:S(2)}) collective-permute-start(bf16[2048,2,128]{2,0,1:T(8,128)(2,1)} %get-tuple-element.404), channel_id=1, source_target_pairs={{0,4},{4,8},{8,12},{12,16},{16,20},{20,24},{24,28},{28,0},{1,5},{5... | collective-permute-start | bytes 3145736 | tf_op jit(solution)/shard_map/while/body/eval_jaxpr/ppermute | solution.py:15
  172.4 1.7 copy-start.3
  188.9 16.2 %collective-permute-start = (bf16[2048,2,128]{2,0,1:T(8,128)(2,1)}, bf16[2048,2,128]{2,0,1:T(8,128)(2,1)S(1)}, u32[]{:S(2)}, u32[]{:S(2)}) collective-permute-start(bf16[2048,2,128]{2,0,1:T(8,128)(2,1)} %get-tuple-element.404), channel_id=1, source_target_pairs={{0,4},{4,8},{8,12},{12,16},{16,20},{20,24},{24,28},{28,0},{1,5},{5... | collective-permute-start | bytes 3145736 | tf_op jit(solution)/shard_map/while/body/eval_jaxpr/ppermute | solution.py:15
  211.0 1.7 copy-start.3
  227.5 16.2 %collective-permute-start = (bf16[2048,2,128]{2,0,1:T(8,128)(2,1)}, bf16[2048,2,128]{2,0,1:T(8,128)(2,1)S(1)}, u32[]{:S(2)}, u32[]{:S(2)}) collective-permute-start(bf16[2048,2,128]{2,0,1:T(8,128)(2,1)} %get-tuple-element.404), channel_id=1, source_target_pairs={{0,4},{4,8},{8,12},{12,16},{16,20},{20,24},{24,28},{28,0},{1,5},{5... | collective-permute-start | bytes 3145736 | tf_op jit(solution)/shard_map/while/body/eval_jaxpr/ppermute | solution.py:15
  249.6 1.7 copy-start.3
  266.1 16.2 %collective-permute-start = (bf16[2048,2,128]{2,0,1:T(8,128)(2,1)}, bf16[2048,2,128]{2,0,1:T(8,128)(2,1)S(1)}, u32[]{:S(2)}, u32[]{:S(2)}) collective-permute-start(bf16[2048,2,128]{2,0,1:T(8,128)(2,1)} %get-tuple-element.404), channel_id=1, source_target_pairs={{0,4},{4,8},{8,12},{12,16},{16,20},{20,24},{24,28},{28,0},{1,5},{5... | collective-permute-start | bytes 3145736 | tf_op jit(solution)/shard_map/while/body/eval_jaxpr/ppermute | solution.py:15
  288.1 1.7 copy-start.3
  304.6 16.2 %collective-permute-start = (bf16[2048,2,128]{2,0,1:T(8,128)(2,1)}, bf16[2048,2,128]{2,0,1:T(8,128)(2,1)S(1)}, u32[]{:S(2)}, u32[]{:S(2)}) collective-permute-start(bf16[2048,2,128]{2,0,1:T(8,128)(2,1)} %get-tuple-element.404), channel_id=1, source_target_pairs={{0,4},{4,8},{8,12},{12,16},{16,20},{20,24},{24,28},{28,0},{1,5},{5... | collective-permute-start | bytes 3145736 | tf_op jit(solution)/shard_map/while/body/eval_jaxpr/ppermute | solution.py:15
  326.7 1.7 copy-start.3
  343.2 36.9 %copy-start.1 = (bf16[512,2,192]{0,2,1:T(8,128)(2,1)S(1)}, bf16[512,2,192]{0,2,1:T(8,128)(2,1)}, u32[]{:S(2)}) copy-start(bf16[512,2,192]{0,2,1:T(8,128)(2,1)} %param.7) | copy-start | bytes 1179652
Sparse Core Ops, SparseCore 0:
  9.2 38.0 all-gather.1
  347.6 32.4 reduce-scatter.1
where the time goes:
time: 388 us; the launch traced here: 387 us
  waiting for transfers between devices  181 us (47%)
  local copies, waits for them, and re-layouts  77.8 us (20%)
  matrix products  77.6 us (20%)
  other arithmetic  36.2 us (9%)
  between operations  13.6 us (4%)
    ppermute x7, waiting for transfers between devices, passed_along(): lax.ppermute(value, axis, [(i, (i + by) % peers) for i in range(peers)])  110 us
    dot_general x8, matrix products, absorb(): jnp.einsum('bhqj,bjhe->bhqe', weights.astype(jnp.bfloat16), kv_tiles[...,...  52.7 us
    gather x16, local copies, waits for them, and re-layouts, gather_tiles(): picked = blocks[chosen]  45.6 us
    all_gather x1, waiting for transfers between devices, per_device(): lax.all_gather(node_feats, 'group', axis=0, tiled=True)  37.5 us
    reduce_scatter x1, waiting for transfers between devices, per_device(): lax.psum_scatter(jnp.dot(mixed, w_out, preferred_element_type=jnp.float32...  32.6 us
    reduce_sum x8, other arithmetic, absorb(): denom = denom * rescale + jnp.sum(weights, axis=-1)  23.6 us
    dot_general x8, matrix products, absorb(): jnp.einsum('bqhe,bjhe->bhqj', queries, kv_tiles[..., :head_dim], preferre...  19.3 us
    slice x8, local copies, waits for them, and re-layouts, absorb(): kv_tiles[..., head_dim:]  14.6 us
  transfers between devices with their start and end apart: 9, of which 9 were waited for; matrix products, arithmetic and copies ran while one was open for 1% of the time, Pallas kernels for 0%

commit v1 on v0

v1 whole, which is shorter than its diff:
```python
import functools

import jax
import jax.numpy as jnp
from jax import lax
from jax.experimental import pallas as pl
from jax.experimental.pallas import tpu as pltpu
from jax.sharding import PartitionSpec as P

TILE = 128
LOG2E = 1.4426950408889634


def attend_kernel(heads, head_dim, cols_ref, q_ref, kv_ref, out_ref):
    row = pl.program_id(0)
    slots = cols_ref.shape[1]
    wide = 2 * head_dim
    factor = LOG2E / head_dim**0.5
    starts = [pl.multiple_of(cols_ref[row, s] * TILE, TILE) for s in range(slots)]
    mixed = []
    for h in range(heads):
        lanes = slice(h * wide, (h + 1) * wide)
        kv = jnp.concatenate([kv_ref[pl.ds(s, TILE), lanes] for s in starts], axis=0)
        scores = lax.dot_general(
            q_ref[:, lanes], kv, (((1,), (1,)), ((), ())), preferred_element_type=jnp.float32
        )
        top = jnp.max(scores, axis=-1, keepdims=True)
        weights = jnp.exp2((scores - top) * factor)
        denom = jnp.sum(weights, axis=-1, keepdims=True)
        summed = jnp.dot(weights.astype(jnp.bfloat16), kv, preferred_element_type=jnp.float32)
        mixed.append((summed / denom)[:, head_dim:])
    out_ref[...] = jnp.concatenate(mixed, axis=1).astype(out_ref.dtype)


def attend(cols, queries, kv, heads, head_dim):
    rows = queries.shape[0]
    grid_spec = pltpu.PrefetchScalarGridSpec(
        num_scalar_prefetch=1,
        grid=(rows // TILE,),
        in_specs=[
            pl.BlockSpec((TILE, queries.shape[1]), lambda i, c: (i, 0)),
            pl.BlockSpec(memory_space=pltpu.VMEM),
        ],
        out_specs=pl.BlockSpec((TILE, heads * head_dim), lambda i, c: (i, 0)),
    )
    return pl.pallas_call(
        functools.partial(attend_kernel, heads, head_dim),
        grid_spec=grid_spec,
        out_shape=jax.ShapeDtypeStruct((rows, heads * head_dim), jnp.bfloat16),
        compiler_params=pltpu.CompilerParams(vmem_limit_bytes=48 * 2**20),
    )(cols, queries, kv)


def project(feats, weight):
    return jnp.dot(feats, weight, preferred_element_type=jnp.float32).astype(jnp.bfloat16)


def per_device(node_feats, w_qkv, w_out, tile_cols):
    width, heads, packed = w_qkv.shape
    head_dim = packed // 3
    feats = lax.all_gather(node_feats, "group", axis=0, tiled=True)
    w_q = jnp.pad(w_qkv[:, :, :head_dim], ((0, 0), (0, 0), (0, head_dim)))
    w_q = w_q.reshape(width, heads * 2 * head_dim)
    w_kv = w_qkv[:, :, head_dim:].reshape(width, heads * 2 * head_dim)
    kv = lax.all_gather(project(feats, w_kv), "loop", axis=0, tiled=True)
    queries = project(feats, w_q)
    w_full = lax.all_gather(w_out, "group", axis=0, tiled=True)
    mixed = attend(tile_cols, queries, kv, heads, head_dim)
    mixed = lax.all_to_all(mixed, "group", split_axis=0, concat_axis=1, tiled=True)
    return jnp.dot(mixed, w_full, preferred_element_type=jnp.float32).astype(jnp.bfloat16)


def solution(mesh):
    placed = (P(("loop", "group"), None), P(None, "group", None), P("group", None), P("loop", None))
    return jax.shard_map(
        per_device,
        mesh=mesh,
        in_specs=placed,
        out_specs=P(("loop", "group"), None),
        check_vma=False,
    )
```

time: 388 us -> 180 us (0.46)
  local copies, waits for them, and re-layouts: 77.8 us -> 1.03 us
  matrix products: 77.6 us -> 5.46 us
  waiting for transfers between devices: 181 us -> 121 us
  other arithmetic: 36.2 us -> 1.13 us
  Pallas kernels: 0 us -> 19.6 us
  blocking collectives: 0 us -> 14.3 us
    ppermute x7 -> x0, waiting for transfers between devices: 110 us -> none  [passed_along(): lax.ppermute(value, axis, [(i, (i + by) % peers) for i in range(peers)])]
    all_gather x1 -> x2, waiting for transfers between devices: 37.5 us -> 120 us  [the longest x1 81.5 us: per_device(): kv = lax.all_gather(project(feats, w_kv), 'loop', axis=0, tiled=True)]
    dot_general x17 -> x3, matrix products: 75 us -> 5.46 us  [the longest x2 4.21 us: project(): jnp.dot(feats, weight, preferred_element_type=jnp.float32)]
    gather x16 -> x0, local copies, waits for them, and re-layouts: 45.6 us -> none  [gather_tiles(): picked = blocks[chosen]]
    reduce_scatter x1 -> x0, waiting for transfers between devices: 32.6 us -> none  [per_device(): lax.psum_scatter(jnp.dot(mixed, w_out, preferred_element_type=jnp.float32...]
    reduce_sum x16 -> x0, other arithmetic: 23.8 us -> none  [the longest x8 23.6 us: absorb(): denom = denom * rescale + jnp.sum(weights, axis=-1)]
    pallas_call x0 -> x1, Pallas kernels: none -> 19.6 us  [attend(): pl.pallas_call(functools.partial(attend_kernel, heads, head_dim), grid_sp...]
    slice x9 -> x0, local copies, waits for them, and re-layouts: 14.7 us -> none  [the longest x8 14.6 us: absorb(): kv_tiles[..., head_dim:]]
  transfers between devices with their start and end apart: 9 -> 3, of which waited for: 9 -> 2; matrix products, arithmetic and copies ran while one was open for 1% -> 1% of each run, Pallas kernels for 0% -> 0%
where the time goes in v1:
time: 180 us
  waiting for transfers between devices  121 us (67%)
  Pallas kernels  19.6 us (11%)
  blocking collectives  14.3 us (8%)
  between operations  13.4 us (7%)
  matrix products  5.46 us (3%)
  starting transfers between devices  3.73 us (2%)
    all_gather x1, waiting for transfers between devices, per_device(): kv = lax.all_gather(project(feats, w_kv), 'loop', axis=0, tiled=True)  81.5 us
    all_gather x1, waiting for transfers between devices, per_device(): feats = lax.all_gather(node_feats, 'group', axis=0, tiled=True)  38.8 us
    pallas_call x1, Pallas kernels, attend(): pl.pallas_call(functools.partial(attend_kernel, heads, head_dim), grid_sp...  19.6 us
    all_gather x1, blocking collectives, per_device(): w_full = lax.all_gather(w_out, 'group', axis=0, tiled=True)  14.3 us
    dot_general x2, matrix products, project(): jnp.dot(feats, weight, preferred_element_type=jnp.float32)  4.21 us
    all_to_all x1, starting transfers between devices, per_device(): lax.all_to_all(mixed, 'group', split_axis=0, concat_axis=1, tiled=True)  3.69 us
  transfers between devices with their start and end apart: 3, of which 2 were waited for; matrix products, arithmetic and copies ran while one was open for 1% of the time, Pallas kernels for 0%

profile of v1, /device:TPU:0, one launch (start us, length us, event | category | flops | bytes accessed | tf_op | source)
XLA Modules:
  0.0 179.7 jit_solution(16222082446221346287)
XLA Ops:
  6.5 0.0 all-gather.3.cloned.1.call-start
  6.5 0.7 all-gather.3.cloned.1.call-update
  7.3 0.0 all-gather.5.cloned.1.call-start
  7.3 1.1 fusion.1
  8.4 38.8 %all-gather.3.cloned.1.call-done = bf16[2048,512]{1,0:T(8,128)(2,1)} async-done(((bf16[512,512]{1,0:T(8,128)(2,1)}), bf16[2048,512]{1,0:T(8,128)(2,1)}) %all-gather.3.cloned.1.call-update) | async-done | bytes 2097168 | tf_op jit(solution)/shard_map/all_gather | solution.py:61
  47.2 0.0 copy-start.1
  47.2 3.5 %convolution_convert_fusion = bf16[2048,256]{1,0:T(8,128)(2,1)} fusion(bf16[2048,512]{1,0:T(8,128)(2,1)} %all-gather.3.cloned.1.call-done, bf16[512,256]{0,1:T(8,128)(2,1)S(1)} %bitcast.16), kind=kOutput, calls=%fused_computation | convolution fusion | flops 537395200 | bytes 3407872 | tf_op jit(solution)/shard_map/dot_general | solution.py:55
  50.7 0.0 copy-start
  50.7 0.0 all-gather.5.cloned.1.call-update
  50.7 0.0 copy-done.1
  50.8 0.7 fusion.q_ref
  51.5 81.5 %all-gather.5.cloned.1.call-done.kv_ref = bf16[16384,256]{1,0:T(8,128)(2,1)} async-done(((bf16[2048,256]{1,0:T(8,128)(2,1)}), bf16[16384,256]{1,0:T(8,128)(2,1)}) %all-gather.5.cloned.1.call-update) | async-done | bytes 8388624 | tf_op jit(solution)/shard_map/all_gather | solution.py:65
  132.9 0.0 copy-done
  133.0 19.6 %shard_map.46 = bf16[2048,128]{1,0:T(8,128)(2,1)S(1)} custom-call(s32[16,10]{1,0:T(8,128)S(1)} %copy-done, bf16[2048,256]{1,0:T(8,128)(2,1)S(1)} %fusion.q_ref, bf16[16384,256]{1,0:T(8,128)(2,1)} %all-gather.5.cloned.1.call-done.kv_ref), custom_call_target="tpu_custom_call" | custom-call | tf_op jit(solution)/shard_map/pallas_call | solution.py:46
  152.6 0.0 copy-start.2
  152.6 1.0 copy.7
  153.6 3.7 %all-to-all-start = ((bf16[4,512,128]{1,2,0:T(8,128)(2,1)}), bf16[4,512,128]{1,2,0:T(8,128)(2,1)S(1)}, u32[]{:S(2)}, u32[]{:S(2)}) async-start(bf16[4,512,128]{1,2,0:T(8,128)(2,1)} %copy.7), calls=%async_computation | async-start | bytes 1048576 | tf_op jit(solution)/shard_map/all_to_all | solution.py:69
  157.3 0.0 copy-done.2
  157.3 14.3 %all_gather.11 = bf16[512,512]{1,0:T(8,128)(2,1)S(1)} all-gather(bf16[128,512]{1,0:T(8,128)(2,1)S(1)} %copy-done.2), channel_id=1, replica_groups=mesh['loop'=8,'group'=4] {'group'}, dimensions={0}, use_global_device_ids=true | all-gather | bytes 655360 | tf_op jit(solution)/shard_map/all_gather | solution.py:67
  171.6 0.0 all-to-all-done
  171.6 1.3 convolution_convert_fusion.2
Async XLA Ops:
  6.5 40.7 %all-gather.3.cloned.1.call-start = ((), (), s32[]{:S(2)}) async-start(), calls=%async_computation.1 | async-start | bytes 2621440 | tf_op jit(solution)/shard_map/all_gather | solution.py:61
  7.3 125.7 %all-gather.5.cloned.1.call-start = ((), (), s32[]{:S(2)}) async-start(), calls=%async_computation.2 | async-start | bytes 9437184 | tf_op jit(solution)/shard_map/all_gather | solution.py:65
  47.2 3.5 %copy-start.1 = (bf16[2048,512]{1,0:T(8,128)(2,1)S(1)}, bf16[2048,512]{1,0:T(8,128)(2,1)}, u32[]{:S(2)}) copy-start(bf16[2048,512]{1,0:T(8,128)(2,1)} %all-gather.3.cloned.1.call-done) | copy-start | bytes 6291460
  50.7 82.2 %copy-start = (s32[16,10]{1,0:T(8,128)S(1)}, s32[16,10]{1,0:T(8,128)}, u32[]{:S(2)}) copy-start(s32[16,10]{1,0:T(8,128)} %cols_ref.1) | copy-start | bytes 1924
  152.6 4.7 %copy-start.2 = (bf16[128,512]{1,0:T(8,128)(2,1)S(1)}, bf16[128,512]{1,0:T(8,128)(2,1)}, u32[]{:S(2)}) copy-start(bf16[128,512]{1,0:T(8,128)(2,1)} %param.6) | copy-start | bytes 393220
  153.6 18.0 %all-to-all-start = ((bf16[4,512,128]{1,2,0:T(8,128)(2,1)}), bf16[4,512,128]{1,2,0:T(8,128)(2,1)S(1)}, u32[]{:S(2)}, u32[]{:S(2)}) async-start(bf16[4,512,128]{1,2,0:T(8,128)(2,1)} %copy.7), calls=%async_computation | async-start | bytes 1048576 | tf_op jit(solution)/shard_map/all_to_all | solution.py:69
Sparse Core Ops, SparseCore 0:
  9.2 38.0 all-gather.2
  50.9 82.0 all-gather.4

commit v2 on v1

--- a/solution.py
+++ b/solution.py
@@ -8,6 +8,7 @@
 from jax.sharding import PartitionSpec as P
 
 TILE = 128
+MESH = pl.DeviceIdType.MESH
 LOG2E = 1.4426950408889634
 
 
@@ -51,20 +52,201 @@
     )(cols, queries, kv)
 
 
-def project(feats, weight):
-    return jnp.dot(feats, weight, preferred_element_type=jnp.float32).astype(jnp.bfloat16)
+def gather_kernel(
+    n_loop, n_group, feats_ref, w_ref, w_out_ref, kv_ref, q_ref, w_full_ref, arrived, own,
+    feat_send, feat_recv, wout_send, wout_recv, up_send, up_recv, down_send, down_recv,
+    sib_send, sib_recv, keep_sem, keep_w_sem,
+):
+    me, g = lax.axis_index("loop"), lax.axis_index("group")
+    core, z = me % 2, me // 2
+    chips = n_loop // 2
+    sib = me + 1 - 2 * core
+    has_up, has_down = z < chips - 1, z > 0
+    rows, wide = own.shape[1], own.shape[2]
+    cut = w_out_ref.shape[0]
+
+    barrier = pltpu.get_barrier_semaphore()
+
+    def greet(device):
+        pl.semaphore_signal(barrier, inc=1, device_id=device, device_id_type=MESH)
+
+    for j in range(1, n_group):
+        greet((me, (g + j) % n_group))
+    greet((sib, g))
+    pl.when(has_up)(lambda: greet((me + 2, g)))
+    pl.when(has_down)(lambda: greet((me - 2, g)))
+    greetings = n_group + jnp.where(has_up, 1, 0) + jnp.where(has_down, 1, 0)
+    pl.semaphore_wait(barrier, greetings)
+
+    def remote(src, dst, send, recv, device):
+        return pltpu.make_async_remote_copy(
+            src_ref=src, dst_ref=dst, send_sem=send, recv_sem=recv,
+            device_id=device, device_id_type=MESH,
+        )
+
+    def feat_copy(j):
+        return remote(
+            feats_ref, arrived.at[n_group - j - 1], feat_send.at[j - 1],
+            feat_recv.at[n_group - j - 1], (me, (g + j) % n_group),
+        )
+
+    def wout_copy(j, owner):
+        part = w_full_ref.at[pl.ds(pl.multiple_of(owner * cut, cut), cut)]
+        return remote(
+            w_out_ref, part, wout_send.at[j - 1], wout_recv.at[n_group - j - 1],
+            (me, (g + j) % n_group),
+        )
+
+    def up_copy(src, block, k, s):
+        dst = kv_ref.at[block, (g + k) % n_group]
+        return remote(
+            dst if src is None else src, dst, up_send.at[s, k], up_recv.at[s, k], (me + 2, g)
+        )
+
+    def down_copy(src, block, k, s):
+        dst = kv_ref.at[block, (g + k) % n_group]
+        return remote(
+            dst if src is None else src, dst, down_send.at[s, k], down_recv.at[s, k], (me - 2, g)
+        )
+
+    def sib_copy(src, block, k, role):
+        dst = kv_ref.at[block, (g + k) % n_group]
+        return remote(
+            dst if src is None else src, dst, sib_send.at[role, k], sib_recv.at[role, k], (sib, g)
+        )
+
+    def keep_copy(k):
+        return pltpu.make_async_copy(
+            own.at[k], kv_ref.at[me, (g + k) % n_group], keep_sem.at[k]
+        )
+
+    for j in range(1, n_group):
+        feat_copy(j).start()
+
+    def own_piece(k):
+        if k:
+            feat_copy(n_group - k).wait_recv()
+        source = feats_ref if k == 0 else arrived.at[k - 1]
+        base = pl.multiple_of(((g + k) % n_group) * rows, rows)
+        step = 256
+
+        @pl.loop(0, rows // step)
+        def _(i):
+            at = pl.multiple_of(i * step, step)
+            both = jnp.dot(
+                source[pl.ds(at, step), :], w_ref[...], preferred_element_type=jnp.float32
+            ).astype(jnp.bfloat16)
+            q_ref[pl.ds(pl.multiple_of(base + at, step), step), :] = both[:, :wide]
+            own[k, pl.ds(at, step), :] = both[:, wide:]
+
+        pl.when(has_up)(lambda: up_copy(own.at[k], me, k, 0).start())
+        pl.when(has_down)(lambda: down_copy(own.at[k], me, k, 0).start())
+        sib_copy(own.at[k], me, k, 0).start()
+        keep_copy(k).start()
+
+    def arrival(k, s):
+        @pl.when(z - 1 - s >= 0)
+        def _():
+            block = me - 2 * (1 + s)
+            up_copy(None, block, k, s).wait_recv()
+            if s + 1 < chips - 1:
+                pl.when(has_up)(lambda: up_copy(None, block, k, s + 1).start())
+            sib_copy(None, block, k, 1 + s).start()
+
+        @pl.when(z + 1 + s < chips)
+        def _():
+            block = me + 2 * (1 + s)
+            down_copy(None, block, k, s).wait_recv()
+            if s + 1 < chips - 1:
+                pl.when(has_down)(lambda: down_copy(None, block, k, s + 1).start())
+            sib_copy(None, block, k, chips + s).start()
+
+    for t in range(n_group + chips - 1):
+        if t < n_group:
+            own_piece(t)
+        if t == n_group - 1:
+            for j in range(1, n_group):
+                wout_copy(j, g).start()
+            keep_w = pltpu.make_async_copy(
+                w_out_ref, w_full_ref.at[pl.ds(pl.multiple_of(g * cut, cut), cut)], keep_w_sem
+            )
+            keep_w.start()
+        for s in range(chips - 1):
+            if 0 <= t - 1 - s < n_group:
+                arrival(t - 1 - s, s)
+
+    keep_w.wait()
+    for j in range(1, n_group):
+        feat_copy(j).wait_send()
+        wout_copy(j, g).wait_send()
+        wout_copy(n_group - j, (g + j) % n_group).wait_recv()
+    for k in range(n_group):
+        keep_copy(k).wait()
+        mine = sib_copy(own.at[k], me, k, 0)
+        mine.wait_send()
+        sib_copy(None, sib, k, 0).wait_recv()
+        for s in range(chips - 1):
+
+            @pl.when(z - 1 - s >= 0)
+            def _():
+                sib_copy(None, me - 2 * (1 + s), k, 1 + s).wait_send()
+                sib_copy(None, sib - 2 * (1 + s), k, 1 + s).wait_recv()
+
+            @pl.when(z + 1 + s < chips)
+            def _():
+                sib_copy(None, me + 2 * (1 + s), k, chips + s).wait_send()
+                sib_copy(None, sib + 2 * (1 + s), k, chips + s).wait_recv()
+
+            @pl.when(has_up & (z - s >= 0))
+            def _():
+                up_copy(own.at[k] if s == 0 else None, me - 2 * s, k, s).wait_send()
+
+            @pl.when(has_down & (z + s < chips))
+            def _():
+                down_copy(own.at[k] if s == 0 else None, me + 2 * s, k, s).wait_send()
+
+
+def gather(feats, weight, w_out, n_loop, n_group):
+    rows, width = feats.shape
+    wide = weight.shape[1] // 2
+    chips = n_loop // 2
+    vmem, anywhere = pl.BlockSpec(memory_space=pltpu.VMEM), pl.BlockSpec(memory_space=pl.ANY)
+    dma = pltpu.SemaphoreType.DMA
+    return pl.pallas_call(
+        functools.partial(gather_kernel, n_loop, n_group),
+        in_specs=[vmem, vmem, anywhere],
+        out_specs=[anywhere, vmem, anywhere],
+        out_shape=[
+            jax.ShapeDtypeStruct((n_loop, n_group, rows, wide), jnp.bfloat16),
+            jax.ShapeDtypeStruct((n_group * rows, wide), jnp.bfloat16),
+            jax.ShapeDtypeStruct((n_group * w_out.shape[0], w_out.shape[1]), jnp.bfloat16),
+        ],
+        scratch_shapes=[
+            pltpu.VMEM((n_group - 1, rows, width), jnp.bfloat16),
+            pltpu.VMEM((n_group, rows, wide), jnp.bfloat16),
+            dma((n_group - 1,)), dma((n_group - 1,)),
+            dma((n_group - 1,)), dma((n_group - 1,)),
+            dma((chips - 1, n_group)), dma((chips - 1, n_group)),
+            dma((chips - 1, n_group)), dma((chips - 1, n_group)),
+            dma((2 * chips - 1, n_group)), dma((2 * chips - 1, n_group)),
+            dma((n_group,)), dma(()),
+        ],
+        compiler_params=pltpu.CompilerParams(
+            collective_id=0, has_side_effects=True, vmem_limit_bytes=48 * 2**20
+        ),
+    )(feats, weight, w_out)
 
 
 def per_device(node_feats, w_qkv, w_out, tile_cols):
     width, heads, packed = w_qkv.shape
     head_dim = packed // 3
-    feats = lax.all_gather(node_feats, "group", axis=0, tiled=True)
+    n_loop, n_group = lax.axis_size("loop"), lax.axis_size("group")
     w_q = jnp.pad(w_qkv[:, :, :head_dim], ((0, 0), (0, 0), (0, head_dim)))
     w_q = w_q.reshape(width, heads * 2 * head_dim)
     w_kv = w_qkv[:, :, head_dim:].reshape(width, heads * 2 * head_dim)
-    kv = lax.all_gather(project(feats, w_kv), "loop", axis=0, tiled=True)
-    queries = project(feats, w_q)
-    w_full = lax.all_gather(w_out, "group", axis=0, tiled=True)
+    weight = jnp.concatenate([w_q, w_kv], axis=1)
+    kv, queries, w_full = gather(node_feats, weight, w_out, n_loop, n_group)
+    kv = kv.reshape(-1, kv.shape[-1])
     mixed = attend(tile_cols, queries, kv, heads, head_dim)
     mixed = lax.all_to_all(mixed, "group", split_axis=0, concat_axis=1, tiled=True)
     return jnp.dot(mixed, w_full, preferred_element_type=jnp.float32).astype(jnp.bfloat16)

time: 180 us -> 132 us (0.73)
  waiting for transfers between devices: 121 us -> 0 us
  Pallas kernels: 19.6 us -> 114 us
  between operations: 13.4 us -> 0.07 us
  matrix products: 5.46 us -> 1.26 us
  starting transfers between devices: 3.73 us -> 0 us
  local copies, waits for them, and re-layouts: 1.03 us -> 3.11 us
  blocking collectives: 14.3 us -> 12.3 us
    all_gather x2 -> x0, waiting for transfers between devices: 120 us -> none  [the longest x1 81.5 us: per_device(): kv = lax.all_gather(project(feats, w_kv), 'loop', axis=0, tiled=True)]
    pallas_call x0 -> x1, Pallas kernels: none -> 94 us  [gather(): pl.pallas_call(functools.partial(gather_kernel, n_loop, n_group), in_spec...]
    all_gather x1 -> x0, blocking collectives: 14.3 us -> none  [per_device(): w_full = lax.all_gather(w_out, 'group', axis=0, tiled=True)]
    all_to_all x0 -> x1, blocking collectives: none -> 12.3 us  [per_device(): lax.all_to_all(mixed, 'group', split_axis=0, concat_axis=1, tiled=True)]
    dot_general x2 -> x0, matrix products: 4.21 us -> none  [project(): jnp.dot(feats, weight, preferred_element_type=jnp.float32)]
    all_to_all x1 -> x0, starting transfers between devices: 3.69 us -> none  [per_device(): lax.all_to_all(mixed, 'group', split_axis=0, concat_axis=1, tiled=True)]
    unnamed x6, local copies, waits for them, and re-layouts: 0.01 us -> 2.63 us
  transfers between devices with their start and end apart: 3 -> 0, of which waited for: 2 -> 0; matrix products, arithmetic and copies ran while one was open for 1% -> 0% of each run, Pallas kernels for 0% -> 0%
where the time goes in v2:
time: 132 us; the launch traced here: 131 us
  Pallas kernels  114 us (86%)
  blocking collectives  12.3 us (9%)
  local copies, waits for them, and re-layouts  3.11 us (2%)
    pallas_call x1, Pallas kernels, gather(): pl.pallas_call(functools.partial(gather_kernel, n_loop, n_group), in_spec...  94 us
    pallas_call x1, Pallas kernels, attend(): pl.pallas_call(functools.partial(attend_kernel, heads, head_dim), grid_sp...  19.6 us
    all_to_all x1, blocking collectives, per_device(): lax.all_to_all(mixed, 'group', split_axis=0, concat_axis=1, tiled=True)  12.3 us

profile of v2, /device:TPU:0, one launch (start us, length us, event | category | flops | bytes accessed | tf_op | source)
XLA Modules:
  0.0 131.5 jit_solution(7611801940800626024)
XLA Ops:
  0.0 1.1 slice_select_fusion
  1.1 0.1 copy.10
  1.3 0.1 copy.11
  1.4 0.0 copy-start
  1.5 1.0 copy-done
  2.5 0.0 copy-start.1
  2.5 0.9 copy-done.1
  3.4 94.0 %shard_map.46 = (bf16[8,4,512,256]{3,2,1,0:T(8,128)(2,1)}, bf16[2048,256]{1,0:T(8,128)(2,1)S(1)}, bf16[512,512]{1,0:T(8,128)(2,1)S(1)}) custom-call(bf16[512,512]{1,0:T(8,128)(2,1)S(1)} %copy-done, bf16[512,512]{1,0:T(8,128)(2,1)S(1)} %pad_maximum_fusion.w_ref, bf16[128,512]{1,0:T(8,128)(2,1)S(1)} %copy-done.1), custom_call_target="tpu_custom_call" | custom-call | tf_op jit(solution)/shard_map/pallas_call | solution.py:215
  97.4 0.0 copy-start.2
  97.4 0.7 copy-done.2
  98.1 19.6 %shard_map.47 = bf16[2048,128]{1,0:T(8,128)(2,1)S(1)} custom-call(s32[16,10]{1,0:T(8,128)S(1)} %copy-done.2, bf16[2048,256]{1,0:T(8,128)(2,1)S(1)} %get-tuple-element.8.q_ref, bf16[16384,256]{1,0:T(8,128)(2,1)} %bitcast.10), custom_call_target="tpu_custom_call" | custom-call | tf_op jit(solution)/shard_map/pallas_call | solution.py:47
  117.6 0.2 copy.9
  117.9 12.3 %all_to_all.19 = bf16[4,512,128]{1,2,0:T(8,128)(2,1)S(1)} all-to-all(bf16[4,512,128]{1,2,0:T(8,128)(2,1)S(1)} %copy.9), channel_id=1, replica_groups=mesh['loop'=8,'group'=4] {'group'}, dimensions={0} | all-to-all | bytes 1048576 | tf_op jit(solution)/shard_map/all_to_all | solution.py:251
  130.2 1.3 convolution_convert_fusion
  (1 shorter events, 0.0 us)
Async XLA Ops:
  1.4 1.0 copy-start
  2.5 0.9 copy-start.1
  97.4 0.7 copy-start.2

commit v3 on v2

--- a/solution.py
+++ b/solution.py
@@ -56,12 +56,15 @@
     n_loop, n_group, feats_ref, w_ref, w_out_ref, kv_ref, q_ref, w_full_ref, arrived, own,
     feat_send, feat_recv, wout_send, wout_recv, up_send, up_recv, down_send, down_recv,
     sib_send, sib_recv, keep_sem, keep_w_sem,
+    far_feats, far_own, far_send, far_recv, far_sib_send, far_sib_recv, far_keep_sem,
 ):
     me, g = lax.axis_index("loop"), lax.axis_index("group")
     core, z = me % 2, me // 2
     chips = n_loop // 2
     sib = me + 1 - 2 * core
     has_up, has_down = z < chips - 1, z > 0
+    at_end = (z == 0) | (z == chips - 1)
+    across = 2 * (chips - 1 - z) + core
     rows, wide = own.shape[1], own.shape[2]
     cut = w_out_ref.shape[0]
 
@@ -75,7 +78,8 @@
     greet((sib, g))
     pl.when(has_up)(lambda: greet((me + 2, g)))
     pl.when(has_down)(lambda: greet((me - 2, g)))
-    greetings = n_group + jnp.where(has_up, 1, 0) + jnp.where(has_down, 1, 0)
+    pl.when(at_end)(lambda: greet((across, g)))
+    greetings = n_group + jnp.where(at_end, 1, 0) + jnp.where(has_up, 1, 0) + jnp.where(has_down, 1, 0)
     pl.semaphore_wait(barrier, greetings)
 
     def remote(src, dst, send, recv, device):
@@ -120,8 +124,62 @@
             own.at[k], kv_ref.at[me, (g + k) % n_group], keep_sem.at[k]
         )
 
+    def across_copy():
+        return remote(
+            feats_ref, far_feats.at[0], far_send.at[0], far_recv.at[0], (across, g)
+        )
+
+    def far_copy(j):
+        return remote(
+            far_feats.at[0], far_feats.at[n_group - j], far_send.at[j],
+            far_recv.at[n_group - j], (me, (g + j) % n_group),
+        )
+
+    def far_sib_copy(block, k):
+        return remote(
+            far_own.at[k], kv_ref.at[block, (g + k) % n_group],
+            far_sib_send.at[k], far_sib_recv.at[k], (sib, g),
+        )
+
+    def far_keep_copy(k):
+        return pltpu.make_async_copy(
+            far_own.at[k], kv_ref.at[across, (g + k) % n_group], far_keep_sem.at[k]
+        )
+
+    def far_share():
+        across_copy().wait_recv()
+        for j in range(1, n_group):
+            far_copy(j).start()
+
+    def far_project():
+        for k in range(n_group):
+            if k:
+                far_copy(n_group - k).wait_recv()
+            step = 256
+
+            @pl.loop(0, rows // step)
+            def _(i):
+                at = pl.multiple_of(i * step, step)
+                far_own[k, pl.ds(at, step), :] = jnp.dot(
+                    far_feats[k, pl.ds(at, step), :], w_ref[:, wide:],
+                    preferred_element_type=jnp.float32,
+                ).astype(jnp.bfloat16)
+
+            far_sib_copy(across, k).start()
+            far_keep_copy(k).start()
+
+    def far_finish():
+        across_copy().wait_send()
+        for j in range(1, n_group):
+            far_copy(j).wait_send()
+        for k in range(n_group):
+            far_keep_copy(k).wait()
+            far_sib_copy(across, k).wait_send()
+            far_sib_copy(across + 1 - 2 * core, k).wait_recv()
+
     for j in range(1, n_group):
         feat_copy(j).start()
+    pl.when(at_end)(lambda: across_copy().start())
 
     def own_piece(k):
         if k:
@@ -149,7 +207,7 @@
         def _():
             block = me - 2 * (1 + s)
             up_copy(None, block, k, s).wait_recv()
-            if s + 1 < chips - 1:
+            if s + 1 < chips - 2:
                 pl.when(has_up)(lambda: up_copy(None, block, k, s + 1).start())
             sib_copy(None, block, k, 1 + s).start()
 
@@ -157,11 +215,11 @@
         def _():
             block = me + 2 * (1 + s)
             down_copy(None, block, k, s).wait_recv()
-            if s + 1 < chips - 1:
+            if s + 1 < chips - 2:
                 pl.when(has_down)(lambda: down_copy(None, block, k, s + 1).start())
             sib_copy(None, block, k, chips + s).start()
 
-    for t in range(n_group + chips - 1):
+    for t in range(n_group + chips - 2):
         if t < n_group:
             own_piece(t)
         if t == n_group - 1:
@@ -171,9 +229,12 @@
                 w_out_ref, w_full_ref.at[pl.ds(pl.multiple_of(g * cut, cut), cut)], keep_w_sem
             )
             keep_w.start()
-        for s in range(chips - 1):
+            pl.when(at_end)(far_share)
+        for s in range(chips - 2):
             if 0 <= t - 1 - s < n_group:
                 arrival(t - 1 - s, s)
+        if t == n_group:
+            pl.when(at_end)(far_project)
 
     keep_w.wait()
     for j in range(1, n_group):
@@ -185,7 +246,7 @@
         mine = sib_copy(own.at[k], me, k, 0)
         mine.wait_send()
         sib_copy(None, sib, k, 0).wait_recv()
-        for s in range(chips - 1):
+        for s in range(chips - 2):
 
             @pl.when(z - 1 - s >= 0)
             def _():
@@ -204,6 +265,8 @@
             @pl.when(has_down & (z + s < chips))
             def _():
                 down_copy(own.at[k] if s == 0 else None, me + 2 * s, k, s).wait_send()
+
+    pl.when(at_end)(far_finish)
 
 
 def gather(feats, weight, w_out, n_loop, n_group):
@@ -230,6 +293,9 @@
             dma((chips - 1, n_group)), dma((chips - 1, n_group)),
             dma((2 * chips - 1, n_group)), dma((2 * chips - 1, n_group)),
             dma((n_group,)), dma(()),
+            pltpu.VMEM((n_group, rows, width), jnp.bfloat16),
+            pltpu.VMEM((n_group, rows, wide), jnp.bfloat16),
+            dma((n_group,)), dma((n_group,)), dma((n_group,)), dma((n_group,)), dma((n_group,)),
         ],
         compiler_params=pltpu.CompilerParams(
             collective_id=0, has_side_effects=True, vmem_limit_bytes=48 * 2**20

time: 132 us -> 112 us (0.85)
  Pallas kernels: 114 us -> 94.3 us
    pallas_call x1, Pallas kernels: 94 us -> 74.7 us  [gather(): pl.pallas_call(functools.partial(gather_kernel, n_loop, n_group), in_spec...]
where the time goes in v3:
time: 112 us
  Pallas kernels  94.3 us (84%)
  blocking collectives  11.7 us (10%)
  local copies, waits for them, and re-layouts  3.11 us (3%)
  matrix products  1.26 us (1%)
  other arithmetic  1.16 us (1%)
    pallas_call x1, Pallas kernels, gather(): pl.pallas_call(functools.partial(gather_kernel, n_loop, n_group), in_spec...  74.7 us
    pallas_call x1, Pallas kernels, attend(): pl.pallas_call(functools.partial(attend_kernel, heads, head_dim), grid_sp...  19.6 us
    all_to_all x1, blocking collectives, per_device(): lax.all_to_all(mixed, 'group', split_axis=0, concat_axis=1, tiled=True)  11.7 us
    unnamed x6, local copies, waits for them, and re-layouts  2.63 us

profile of v3, /device:TPU:0, one launch (start us, length us, event | category | flops | bytes accessed | tf_op | source)
XLA Modules:
  0.0 111.6 jit_solution(682518981156613076)
XLA Ops:
  0.0 1.1 %slice_select_fusion = (bf16[512,2,128]{0,2,1:T(8,128)(2,1)S(1)}, bf16[512,2,128]{0,2,1:T(8,128)(2,1)S(1)}) fusion(bf16[512,2,192]{0,2,1:T(8,128)(2,1)} %param.5, pred[128]{0:T(512)(128)(4,1)} %constant.3.clone.1), kind=kLoop, calls=%fused_computation.2 | loop fusion | flops 131072 | bytes 1048704 | tf_op jit(solution)/shard_map/jit(_pad)/pad | solution.py:310
  1.1 0.1 copy.10
  1.3 0.1 copy.11
  1.4 0.0 copy-start
  1.5 1.0 copy-done
  2.5 0.0 copy-start.1
  2.5 0.9 copy-done.1
  3.4 74.7 %shard_map.46 = (bf16[8,4,512,256]{3,2,1,0:T(8,128)(2,1)}, bf16[2048,256]{1,0:T(8,128)(2,1)S(1)}, bf16[512,512]{1,0:T(8,128)(2,1)S(1)}) custom-call(bf16[512,512]{1,0:T(8,128)(2,1)S(1)} %copy-done, bf16[512,512]{1,0:T(8,128)(2,1)S(1)} %pad_maximum_fusion.w_ref, bf16[128,512]{1,0:T(8,128)(2,1)S(1)} %copy-done.1), custom_call_target="tpu_custom_call" | custom-call | tf_op jit(solution)/shard_map/pallas_call | solution.py:278
  78.1 0.0 copy-start.2
  78.1 0.7 copy-done.2
  78.8 19.6 %shard_map.47 = bf16[2048,128]{1,0:T(8,128)(2,1)S(1)} custom-call(s32[16,10]{1,0:T(8,128)S(1)} %copy-done.2, bf16[2048,256]{1,0:T(8,128)(2,1)S(1)} %get-tuple-element.8.q_ref, bf16[16384,256]{1,0:T(8,128)(2,1)} %bitcast.10), custom_call_target="tpu_custom_call" | custom-call | tf_op jit(solution)/shard_map/pallas_call | solution.py:47
  98.4 0.2 copy.9
  98.6 11.7 %all_to_all.19 = bf16[4,512,128]{1,2,0:T(8,128)(2,1)S(1)} all-to-all(bf16[4,512,128]{1,2,0:T(8,128)(2,1)S(1)} %copy.9), channel_id=1, replica_groups=mesh['loop'=8,'group'=4] {'group'}, dimensions={0} | all-to-all | bytes 1048576 | tf_op jit(solution)/shard_map/all_to_all | solution.py:317
  110.4 1.3 %convolution_convert_fusion = bf16[512,512]{1,0:T(8,128)(2,1)} fusion(bf16[512,512]{0,1:T(8,128)(2,1)S(1)} %bitcast.13, bf16[512,512]{1,0:T(8,128)(2,1)S(1)} %get-tuple-element.10), kind=kOutput, calls=%fused_computation | convolution fusion | flops 268697600 | bytes 1572864 | tf_op jit(solution)/shard_map/dot_general | solution.py:318
  (1 shorter events, 0.0 us)
Async XLA Ops:
  1.4 1.0 copy-start
  2.5 0.9 copy-start.1
  78.1 0.7 copy-start.2

commit v4 on v3

v4 whole, which is shorter than its diff:
```python
import functools

import jax
import jax.numpy as jnp
from jax import lax
from jax.experimental import pallas as pl
from jax.experimental.pallas import tpu as pltpu
from jax.sharding import PartitionSpec as P

TILE = 128
MESH = pl.DeviceIdType.MESH
LOG2E = 1.4426950408889634


def attend_tile(cols_ref, row, queries, kv_ref, heads, head_dim):
    slots = cols_ref.shape[1]
    wide = 2 * head_dim
    factor = LOG2E / head_dim**0.5
    tiles = [cols_ref[row, s] for s in range(slots)]
    mixed = []
    for h in range(heads):
        lanes = slice(h * wide, (h + 1) * wide)
        kv = jnp.concatenate([kv_ref[t, :, lanes] for t in tiles], axis=0)
        scores = lax.dot_general(
            queries[:, lanes], kv, (((1,), (1,)), ((), ())), preferred_element_type=jnp.float32
        )
        top = jnp.max(scores, axis=-1, keepdims=True)
        weights = jnp.exp2((scores - top) * factor)
        denom = jnp.sum(weights, axis=-1, keepdims=True)
        summed = jnp.dot(weights.astype(jnp.bfloat16), kv, preferred_element_type=jnp.float32)
        mixed.append((summed / denom)[:, head_dim:])
    return jnp.concatenate(mixed, axis=1).astype(jnp.bfloat16)


def fused_kernel(
    n_loop, n_group, heads, head_dim,
    cols_ref, feats_ref, w_ref, w_out_ref, out_ref, kv_ref, q_ref, w_full_ref, arrived,
    feat_send, feat_recv, wout_send, wout_recv, up_send, up_recv, down_send, down_recv,
    sib_send, sib_recv, far_feats, far_send, far_recv, far_sib_send, far_sib_recv,
    mine, landed, mix_send, mix_recv,
):
    me, g = lax.axis_index("loop"), lax.axis_index("group")
    core, z = me % 2, me // 2
    chips = n_loop // 2
    sib = me + 1 - 2 * core
    has_up, has_down = z < chips - 1, z > 0
    at_end = (z == 0) | (z == chips - 1)
    across = 2 * (chips - 1 - z) + core
    rows, wide = feats_ref.shape[0], kv_ref.shape[2]
    cut = w_out_ref.shape[0]

    barrier = pltpu.get_barrier_semaphore()

    def greet(device):
        pl.semaphore_signal(barrier, inc=1, device_id=device, device_id_type=MESH)

    for j in range(1, n_group):
        greet((me, (g + j) % n_group))
    greet((sib, g))
    pl.when(has_up)(lambda: greet((me + 2, g)))
    pl.when(has_down)(lambda: greet((me - 2, g)))
    pl.when(at_end)(lambda: greet((across, g)))
    greetings = n_group + jnp.where(at_end, 1, 0) + jnp.where(has_up, 1, 0) + jnp.where(has_down, 1, 0)
    pl.semaphore_wait(barrier, greetings)

    def remote(src, dst, send, recv, device):
        return pltpu.make_async_remote_copy(
            src_ref=src, dst_ref=dst, send_sem=send, recv_sem=recv,
            device_id=device, device_id_type=MESH,
        )

    def place(block, k):
        return (block * n_group + (g + k) % n_group) * (rows // TILE)

    def piece(block, k):
        return kv_ref.at[pl.ds(place(block, k), rows // TILE)]

    def feat_copy(j):
        return remote(
            feats_ref, arrived.at[n_group - j - 1], feat_send.at[j - 1],
            feat_recv.at[n_group - j - 1], (me, (g + j) % n_group),
        )

    def wout_copy(j, owner):
        part = w_full_ref.at[pl.ds(pl.multiple_of(owner * cut, cut), cut)]
        return remote(
            w_out_ref, part, wout_send.at[j - 1], wout_recv.at[n_group - j - 1],
            (me, (g + j) % n_group),
        )

    def up_copy(block, k, s):
        at = piece(block, k)
        return remote(at, at, up_send.at[s, k], up_recv.at[s, k], (me + 2, g))

    def down_copy(block, k, s):
        at = piece(block, k)
        return remote(at, at, down_send.at[s, k], down_recv.at[s, k], (me - 2, g))

    def sib_copy(block, k, role):
        at = piece(block, k)
        return remote(at, at, sib_send.at[role, k], sib_recv.at[role, k], (sib, g))

    def across_copy():
        return remote(
            feats_ref, far_feats.at[0], far_send.at[0], far_recv.at[0], (across, g)
        )

    def far_copy(j):
        return remote(
            far_feats.at[0], far_feats.at[n_group - j], far_send.at[j],
            far_recv.at[n_group - j], (me, (g + j) % n_group),
        )

    def far_sib_copy(block, k):
        at = piece(block, k)
        return remote(at, at, far_sib_send.at[k], far_sib_recv.at[k], (sib, g))

    def far_share():
        across_copy().wait_recv()
        for j in range(1, n_group):
            far_copy(j).start()

    def far_project():
        for k in range(n_group):
            if k:
                far_copy(n_group - k).wait_recv()
            step = 256

            @pl.loop(0, rows // step)
            def _(i):
                at = pl.multiple_of(i * step, step)
                found = jnp.dot(
                    far_feats[k, pl.ds(at, step), :], w_ref[:, wide:],
                    preferred_element_type=jnp.float32,
                ).astype(jnp.bfloat16)
                for m in range(step // TILE):
                    tile = place(across, k) + i * (step // TILE) + m
                    kv_ref[tile] = found[m * TILE : (m + 1) * TILE]

            far_sib_copy(across, k).start()

    def far_finish():
        across_copy().wait_send()
        for j in range(1, n_group):
            far_copy(j).wait_send()
        for k in range(n_group):
            far_sib_copy(across, k).wait_send()
            far_sib_copy(across + 1 - 2 * core, k).wait_recv()

    for j in range(1, n_group):
        feat_copy(j).start()
    pl.when(at_end)(lambda: across_copy().start())

    def own_piece(k):
        if k:
            feat_copy(n_group - k).wait_recv()
        source = feats_ref if k == 0 else arrived.at[k - 1]
        base = pl.multiple_of(((g + k) % n_group) * rows, rows)
        step = 256

        @pl.loop(0, rows // step)
        def _(i):
            at = pl.multiple_of(i * step, step)
            both = jnp.dot(
                source[pl.ds(at, step), :], w_ref[...], preferred_element_type=jnp.float32
            ).astype(jnp.bfloat16)
            q_ref[pl.ds(pl.multiple_of(base + at, step), step), :] = both[:, :wide]
            for m in range(step // TILE):
                tile = place(me, k) + i * (step // TILE) + m
                kv_ref[tile] = both[m * TILE : (m + 1) * TILE, wide:]

        pl.when(has_up)(lambda: up_copy(me, k, 0).start())
        pl.when(has_down)(lambda: down_copy(me, k, 0).start())
        sib_copy(me, k, 0).start()

    def arrival(k, s):
        @pl.when(z - 1 - s >= 0)
        def _():
            block = me - 2 * (1 + s)
            up_copy(block, k, s).wait_recv()
            if s + 1 < chips - 2:
                pl.when(has_up)(lambda: up_copy(block, k, s + 1).start())
            sib_copy(block, k, 1 + s).start()

        @pl.when(z + 1 + s < chips)
        def _():
            block = me + 2 * (1 + s)
            down_copy(block, k, s).wait_recv()
            if s + 1 < chips - 2:
                pl.when(has_down)(lambda: down_copy(block, k, s + 1).start())
            sib_copy(block, k, chips + s).start()

    for t in range(n_group + chips - 2):
        if t < n_group:
            own_piece(t)
        if t == n_group - 1:
            for j in range(1, n_group):
                wout_copy(j, g).start()
            w_full_ref[pl.ds(pl.multiple_of(g * cut, cut), cut), :] = w_out_ref[...]
            pl.when(at_end)(far_share)
        for s in range(chips - 2):
            if 0 <= t - 1 - s < n_group:
                arrival(t - 1 - s, s)
        if t == n_group:
            pl.when(at_end)(far_project)

    for j in range(1, n_group):
        feat_copy(j).wait_send()
        wout_copy(j, g).wait_send()
        wout_copy(n_group - j, (g + j) % n_group).wait_recv()
    for k in range(n_group):
        sib_copy(me, k, 0).wait_send()
        sib_copy(sib, k, 0).wait_recv()
        for s in range(chips - 2):

            @pl.when(z - 1 - s >= 0)
            def _():
                sib_copy(me - 2 * (1 + s), k, 1 + s).wait_send()
                sib_copy(sib - 2 * (1 + s), k, 1 + s).wait_recv()

            @pl.when(z + 1 + s < chips)
            def _():
                sib_copy(me + 2 * (1 + s), k, chips + s).wait_send()
                sib_copy(sib + 2 * (1 + s), k, chips + s).wait_recv()

            @pl.when(has_up & (z - s >= 0))
            def _():
                up_copy(me - 2 * s, k, s).wait_send()

            @pl.when(has_down & (z + s < chips))
            def _():
                down_copy(me + 2 * s, k, s).wait_send()

    pl.when(at_end)(far_finish)

    def mix_copy(j, slot):
        return remote(
            mine.at[j - 1], landed.at[slot], mix_send.at[j - 1],
            mix_recv.at[n_group - j - 1], (me, (g + j) % n_group),
        )

    for j in [*range(1, n_group), 0]:
        first = ((g + j) % n_group) * (rows // TILE)

        @pl.loop(0, rows // TILE)
        def _(i):
            row = first + i
            at = pl.multiple_of(i * TILE, TILE)
            queries = q_ref[pl.ds(pl.multiple_of(row * TILE, TILE), TILE), :]
            mixed = attend_tile(cols_ref, row, queries, kv_ref, heads, head_dim)
            if j:
                mine[j - 1, pl.ds(at, TILE), :] = mixed
            else:
                landed[g, pl.ds(at, TILE), :] = mixed

        if j:
            mix_copy(j, g).start()

    for j in range(1, n_group):
        mix_copy(j, g).wait_send()
        mix_copy(n_group - j, (g + j) % n_group).wait_recv()

    @pl.loop(0, rows // 256)
    def _(i):
        at = pl.ds(pl.multiple_of(i * 256, 256), 256)
        mixed = jnp.concatenate([landed[m, at, :] for m in range(n_group)], axis=1)
        out_ref[at, :] = jnp.dot(
            mixed, w_full_ref[...], preferred_element_type=jnp.float32
        ).astype(out_ref.dtype)


def fused(cols, feats, weight, w_out, n_loop, n_group, heads, head_dim):
    rows, width = feats.shape
    wide = weight.shape[1] // 2
    chips = n_loop // 2
    vmem, dma = pl.BlockSpec(memory_space=pltpu.VMEM), pltpu.SemaphoreType.DMA
    return pl.pallas_call(
        functools.partial(fused_kernel, n_loop, n_group, heads, head_dim),
        in_specs=[pl.BlockSpec(memory_space=pltpu.SMEM), vmem, vmem, vmem],
        out_specs=vmem,
        out_shape=jax.ShapeDtypeStruct((rows, w_out.shape[1]), jnp.bfloat16),
        scratch_shapes=[
            pltpu.VMEM((n_loop * n_group * rows // TILE, TILE, wide), jnp.bfloat16),
            pltpu.VMEM((n_group * rows, wide), jnp.bfloat16),
            pltpu.VMEM((n_group * w_out.shape[0], w_out.shape[1]), jnp.bfloat16),
            pltpu.VMEM((n_group - 1, rows, width), jnp.bfloat16),
            dma((n_group - 1,)), dma((n_group - 1,)),
            dma((n_group - 1,)), dma((n_group - 1,)),
            dma((chips - 1, n_group)), dma((chips - 1, n_group)),
            dma((chips - 1, n_group)), dma((chips - 1, n_group)),
            dma((2 * chips - 1, n_group)), dma((2 * chips - 1, n_group)),
            pltpu.VMEM((n_group, rows, width), jnp.bfloat16),
            dma((n_group,)), dma((n_group,)), dma((n_group,)), dma((n_group,)),
            pltpu.VMEM((n_group - 1, rows, heads * head_dim), jnp.bfloat16),
            pltpu.VMEM((n_group, rows, heads * head_dim), jnp.bfloat16),
            dma((n_group - 1,)), dma((n_group - 1,)),
        ],
        compiler_params=pltpu.CompilerParams(
            collective_id=0, has_side_effects=True, vmem_limit_bytes=56 * 2**20
        ),
    )(cols, feats, weight, w_out)


def per_device(node_feats, w_qkv, w_out, tile_cols):
    width, heads, packed = w_qkv.shape
    head_dim = packed // 3
    n_loop, n_group = lax.axis_size("loop"), lax.axis_size("group")
    w_q = jnp.pad(w_qkv[:, :, :head_dim], ((0, 0), (0, 0), (0, head_dim)))
    w_q = w_q.reshape(width, heads * 2 * head_dim)
    w_kv = w_qkv[:, :, head_dim:].reshape(width, heads * 2 * head_dim)
    weight = jnp.concatenate([w_q, w_kv], axis=1)
    return fused(tile_cols, node_feats, weight, w_out, n_loop, n_group, heads, head_dim)


def solution(mesh):
    placed = (P(("loop", "group"), None), P(None, "group", None), P("group", None), P("loop", None))
    return jax.shard_map(
        per_device,
        mesh=mesh,
        in_specs=placed,
        out_specs=P(("loop", "group"), None),
        check_vma=False,
    )
```

time: 112 us -> 98.4 us (0.88)
  blocking collectives: 11.7 us -> 0 us
  matrix products: 1.26 us -> 0 us
    all_to_all x1 -> x0, blocking collectives: 11.7 us -> none  [per_device(): lax.all_to_all(mixed, 'group', split_axis=0, concat_axis=1, tiled=True)]
    dot_general x1 -> x0, matrix products: 1.26 us -> none  [per_device(): jnp.dot(mixed, w_full, preferred_element_type=jnp.float32)]
    unnamed x6 -> x1, local copies, waits for them, and re-layouts: 2.63 us -> 1.87 us
    pallas_call x2 -> x1, Pallas kernels: 94.3 us -> 94.1 us  [fused(): pl.pallas_call(functools.partial(fused_kernel, n_loop, n_group, heads, he...]
where the time goes in v4:
time: 98.4 us; the launch traced here: 98.2 us
  Pallas kernels  94.1 us (96%)
  local copies, waits for them, and re-layouts  2.13 us (2%)
  other arithmetic  1.95 us (2%)
    pallas_call x1, Pallas kernels, fused(): pl.pallas_call(functools.partial(fused_kernel, n_loop, n_group, heads, he...  94.1 us

profile of v4, /device:TPU:0, one launch (start us, length us, event | category | flops | bytes accessed | tf_op | source)
XLA Modules:
  0.0 98.2 jit_solution(18161427975839341303)
XLA Ops:
  0.0 1.1 %slice_select_fusion = (bf16[512,2,128]{0,2,1:T(8,128)(2,1)S(1)}, bf16[512,2,128]{0,2,1:T(8,128)(2,1)S(1)}) fusion(bf16[512,2,192]{0,2,1:T(8,128)(2,1)} %param.5, pred[128]{0:T(512)(128)(4,1)} %constant.3.clone.1), kind=kLoop, calls=%fused_computation.1 | loop fusion | flops 131072 | bytes 1048704 | tf_op jit(solution)/shard_map/jit(_pad)/pad | solution.py:308
  1.1 0.1 copy.7
  1.3 0.1 copy.8
  1.4 0.8 pad_maximum_fusion.w_ref
  2.2 94.1 %shard_map.46 = bf16[512,512]{1,0:T(8,128)(2,1)} custom-call(s32[16,10]{1,0:T(8,128)} %cols_ref.1, bf16[512,512]{1,0:T(8,128)(2,1)} %feats_ref.1, bf16[512,512]{1,0:T(8,128)(2,1)} %pad_maximum_fusion.w_ref, bf16[128,512]{1,0:T(8,128)(2,1)} %w_out_ref.1), custom_call_target="tpu_custom_call" | custom-call | tf_op jit(solution)/shard_map/pallas_call | solution.py:277
  96.3 1.9 %copy.10 = bf16[512,512]{1,0:T(8,128)(2,1)} copy(bf16[512,512]{1,0:T(8,128)(2,1)} %shard_map.46) | data formatting | bytes 1048576

commit v5 on v4

--- a/solution.py
+++ b/solution.py
@@ -242,7 +242,7 @@
     for j in [*range(1, n_group), 0]:
         first = ((g + j) % n_group) * (rows // TILE)
 
-        @pl.loop(0, rows // TILE)
+        @pl.loop(0, rows // TILE, unroll=2)
         def _(i):
             row = first + i
             at = pl.multiple_of(i * TILE, TILE)

time: 98.4 us -> 97.3 us (0.989)
  Pallas kernels: 94.1 us -> 93 us
    pallas_call x1, Pallas kernels: 94.1 us -> 93 us  [fused(): pl.pallas_call(functools.partial(fused_kernel, n_loop, n_group, heads, he...]
where the time goes in v5:
time: 97.3 us; the launch traced here: 97.1 us
  Pallas kernels  93 us (96%)
  local copies, waits for them, and re-layouts  2.13 us (2%)
  other arithmetic  1.95 us (2%)
    pallas_call x1, Pallas kernels, fused(): pl.pallas_call(functools.partial(fused_kernel, n_loop, n_group, heads, he...  93 us

profile of v5, /device:TPU:0, one launch (start us, length us, event | category | flops | bytes accessed | tf_op | source)
XLA Modules:
  0.0 97.1 jit_solution(1564352053075009606)
XLA Ops:
  0.0 1.1 %slice_select_fusion = (bf16[512,2,128]{0,2,1:T(8,128)(2,1)S(1)}, bf16[512,2,128]{0,2,1:T(8,128)(2,1)S(1)}) fusion(bf16[512,2,192]{0,2,1:T(8,128)(2,1)} %param.5, pred[128]{0:T(512)(128)(4,1)} %constant.3.clone.1), kind=kLoop, calls=%fused_computation.1 | loop fusion | flops 131072 | bytes 1048704 | tf_op jit(solution)/shard_map/jit(_pad)/pad | solution.py:308
  1.1 0.1 copy.7
  1.3 0.1 copy.8
  1.4 0.8 pad_maximum_fusion.w_ref
  2.2 93.0 %shard_map.46 = bf16[512,512]{1,0:T(8,128)(2,1)} custom-call(s32[16,10]{1,0:T(8,128)} %cols_ref.1, bf16[512,512]{1,0:T(8,128)(2,1)} %feats_ref.1, bf16[512,512]{1,0:T(8,128)(2,1)} %pad_maximum_fusion.w_ref, bf16[128,512]{1,0:T(8,128)(2,1)} %w_out_ref.1), custom_call_target="tpu_custom_call" | custom-call | tf_op jit(solution)/shard_map/pallas_call | solution.py:277
  95.2 1.9 %copy.10 = bf16[512,512]{1,0:T(8,128)(2,1)} copy(bf16[512,512]{1,0:T(8,128)(2,1)} %shard_map.46) | data formatting | bytes 1048576

commit v6 on v5

--- a/solution.py
+++ b/solution.py
@@ -34,7 +34,7 @@
 
 def fused_kernel(
     n_loop, n_group, heads, head_dim,
-    cols_ref, feats_ref, w_ref, w_out_ref, out_ref, kv_ref, q_ref, w_full_ref, arrived,
+    cols_ref, feats_ref, w_ref, w_out_ref, out_ref, whole_ref, kv_ref, q_ref, w_full_ref, arrived,
     feat_send, feat_recv, wout_send, wout_recv, up_send, up_recv, down_send, down_recv,
     sib_send, sib_recv, far_feats, far_send, far_recv, far_sib_send, far_sib_recv,
     mine, landed, mix_send, mix_recv,
@@ -263,10 +263,12 @@
     @pl.loop(0, rows // 256)
     def _(i):
         at = pl.ds(pl.multiple_of(i * 256, 256), 256)
-        mixed = jnp.concatenate([landed[m, at, :] for m in range(n_group)], axis=1)
-        out_ref[at, :] = jnp.dot(
-            mixed, w_full_ref[...], preferred_element_type=jnp.float32
-        ).astype(out_ref.dtype)
+        out_ref[at, :] = jnp.concatenate([landed[m, at, :] for m in range(n_group)], axis=1)
+
+    @pl.loop(0, n_group)
+    def _(i):
+        at = pl.ds(pl.multiple_of(i * cut, cut), cut)
+        whole_ref[at, :] = w_full_ref[at, :]
 
 
 def fused(cols, feats, weight, w_out, n_loop, n_group, heads, head_dim):
@@ -277,8 +279,11 @@
     return pl.pallas_call(
         functools.partial(fused_kernel, n_loop, n_group, heads, head_dim),
         in_specs=[pl.BlockSpec(memory_space=pltpu.SMEM), vmem, vmem, vmem],
-        out_specs=vmem,
-        out_shape=jax.ShapeDtypeStruct((rows, w_out.shape[1]), jnp.bfloat16),
+        out_specs=[vmem, vmem],
+        out_shape=[
+            jax.ShapeDtypeStruct((rows, n_group * heads * head_dim), jnp.bfloat16),
+            jax.ShapeDtypeStruct((n_group * w_out.shape[0], w_out.shape[1]), jnp.bfloat16),
+        ],
         scratch_shapes=[
             pltpu.VMEM((n_loop * n_group * rows // TILE, TILE, wide), jnp.bfloat16),
             pltpu.VMEM((n_group * rows, wide), jnp.bfloat16),
@@ -309,7 +314,10 @@
     w_q = w_q.reshape(width, heads * 2 * head_dim)
     w_kv = w_qkv[:, :, head_dim:].reshape(width, heads * 2 * head_dim)
     weight = jnp.concatenate([w_q, w_kv], axis=1)
-    return fused(tile_cols, node_feats, weight, w_out, n_loop, n_group, heads, head_dim)
+    mixed, w_full = fused(
+        tile_cols, node_feats, weight, w_out, n_loop, n_group, heads, head_dim
+    )
+    return jnp.dot(mixed, w_full, preferred_element_type=jnp.float32).astype(jnp.bfloat16)
 
 
 def solution(mesh):

time: 97.3 us -> 97.5 us (level)
  matrix products: 0 us -> 2.43 us
  local copies, waits for them, and re-layouts: 2.13 us -> 0.27 us
    dot_general x0 -> x1, matrix products: none -> 2.43 us  [per_device(): jnp.dot(mixed, w_full, preferred_element_type=jnp.float32)]
    unnamed x1 -> x0, local copies, waits for them, and re-layouts: 1.87 us -> none
where the time goes in v6:
time: 97.5 us; the launch traced here: 97.4 us
  Pallas kernels  92.7 us (95%)
  matrix products  2.43 us (2%)
  other arithmetic  1.95 us (2%)
    pallas_call x1, Pallas kernels, fused(): pl.pallas_call(functools.partial(fused_kernel, n_loop, n_group, heads, he...  92.7 us
    dot_general x1, matrix products, per_device(): jnp.dot(mixed, w_full, preferred_element_type=jnp.float32)  2.43 us

profile of v6, /device:TPU:0, one launch (start us, length us, event | category | flops | bytes accessed | tf_op | source)
XLA Modules:
  0.0 97.4 jit_solution(11462121235854599107)
XLA Ops:
  0.0 1.1 %slice_select_fusion = (bf16[512,2,128]{0,2,1:T(8,128)(2,1)S(1)}, bf16[512,2,128]{0,2,1:T(8,128)(2,1)S(1)}) fusion(bf16[512,2,192]{0,2,1:T(8,128)(2,1)} %param.5, pred[128]{0:T(512)(128)(4,1)} %constant.3.clone.1), kind=kLoop, calls=%fused_computation.2 | loop fusion | flops 131072 | bytes 1048704 | tf_op jit(solution)/shard_map/jit(_pad)/pad | solution.py:313
  1.1 0.1 copy.7
  1.3 0.1 copy.8
  1.4 0.8 pad_maximum_fusion.w_ref
  2.2 92.7 %shard_map.46 = (bf16[512,512]{1,0:T(8,128)(2,1)}, bf16[512,512]{1,0:T(8,128)(2,1)}) custom-call(s32[16,10]{1,0:T(8,128)} %cols_ref.1, bf16[512,512]{1,0:T(8,128)(2,1)} %feats_ref.1, bf16[512,512]{1,0:T(8,128)(2,1)} %pad_maximum_fusion.w_ref, bf16[128,512]{1,0:T(8,128)(2,1)} %w_out_ref.1), custom_call_target="tpu_custom_call" | custom-call | tf_op jit(solution)/shard_map/pallas_call | solution.py:279
  94.9 2.4 %convolution_convert_fusion = bf16[512,512]{1,0:T(8,128)(2,1)} fusion(bf16[512,512]{1,0:T(8,128)(2,1)} %get-tuple-element.7, bf16[512,512]{1,0:T(8,128)(2,1)} %get-tuple-element.8), kind=kOutput, calls=%fused_computation | convolution fusion | flops 268697600 | bytes 1572864 | tf_op jit(solution)/shard_map/dot_general | solution.py:320

commit v7 on v5

--- a/solution.py
+++ b/solution.py
@@ -242,7 +242,7 @@
     for j in [*range(1, n_group), 0]:
         first = ((g + j) % n_group) * (rows // TILE)
 
-        @pl.loop(0, rows // TILE, unroll=2)
+        @pl.loop(0, rows // TILE, unroll=4)
         def _(i):
             row = first + i
             at = pl.multiple_of(i * TILE, TILE)

time: 97.3 us -> 96.8 us (level)
  no operation moved by 1% of the time
where the time goes in v7:
time: 96.8 us; the launch traced here: 96.6 us
  Pallas kernels  92.5 us (96%)
  local copies, waits for them, and re-layouts  2.13 us (2%)
  other arithmetic  1.95 us (2%)
    pallas_call x1, Pallas kernels, fused(): pl.pallas_call(functools.partial(fused_kernel, n_loop, n_group, heads, he...  92.5 us

profile of v7, /device:TPU:0, one launch (start us, length us, event | category | flops | bytes accessed | tf_op | source)
XLA Modules:
  0.0 96.6 jit_solution(12519674193217691203)
XLA Ops:
  0.0 1.1 %slice_select_fusion = (bf16[512,2,128]{0,2,1:T(8,128)(2,1)S(1)}, bf16[512,2,128]{0,2,1:T(8,128)(2,1)S(1)}) fusion(bf16[512,2,192]{0,2,1:T(8,128)(2,1)} %param.5, pred[128]{0:T(512)(128)(4,1)} %constant.3.clone.1), kind=kLoop, calls=%fused_computation.1 | loop fusion | flops 131072 | bytes 1048704 | tf_op jit(solution)/shard_map/jit(_pad)/pad | solution.py:308
  1.1 0.1 copy.7
  1.3 0.1 copy.8
  1.4 0.8 pad_maximum_fusion.w_ref
  2.2 92.5 %shard_map.46 = bf16[512,512]{1,0:T(8,128)(2,1)} custom-call(s32[16,10]{1,0:T(8,128)} %cols_ref.1, bf16[512,512]{1,0:T(8,128)(2,1)} %feats_ref.1, bf16[512,512]{1,0:T(8,128)(2,1)} %pad_maximum_fusion.w_ref, bf16[128,512]{1,0:T(8,128)(2,1)} %w_out_ref.1), custom_call_target="tpu_custom_call" | custom-call | tf_op jit(solution)/shard_map/pallas_call | solution.py:277
  94.8 1.9 %copy.10 = bf16[512,512]{1,0:T(8,128)(2,1)} copy(bf16[512,512]{1,0:T(8,128)(2,1)} %shard_map.46) | data formatting | bytes 1048576
